TPU v7x, 512 devices: a whole 4x8x8 slice. The times are simulated.
512 devices in a mesh: frames: 16 (over z_lo, x, core), heads: 32 (over z_hi, y).
Axes of the slice: x: 4, y: 8, z: 8 (z_hi: 4, z_lo: 2; z = z_hi * 2 + z_lo), core: 2. Of those that a mesh axis runs over, the one named last changes fastest.
Arguments:
- queries: bfloat16 [4096, 4096], P('frames', 'heads'), may hold values from -6 to 6
- local_keys: bfloat16 [4096, 4096], P('frames', 'heads'), may hold values from -6 to 6
- local_values: bfloat16 [4096, 4096], P('frames', 'heads'), may hold values from -6 to 6
- cache_keys: bfloat16 [32, 512, 4096], P('frames', None, 'heads'), may hold values from -6 to 6
- cache_values: bfloat16 [32, 512, 4096], P('frames', None, 'heads'), may hold values from -6 to 6
- windows: int32 [16, 4], replicated, may hold values from 0 to 31, as said below
- counts: int32 [16], replicated, may hold values from 1 to 4, as said below
- slot_of: int32 [32], replicated, may hold values from 0 to 31, as said below
- residual: bfloat16 [5120, 4096], P('heads', 'frames'), may hold values from -6 to 6
- out_weight: bfloat16 [5120, 4096], P('heads'), may hold values from -0.09375 to 0.09375
- gate_table: float32 [50, 5120], P(None, 'heads'), may hold values from -4 to 4
- timestep: int32 [1], replicated, may hold values from 0 to 49
Outputs:
- updated: bfloat16 [5120, 4096], P('heads', 'frames')
Inputs may be any that keep to these rules, and one draw needn't show every extreme that they name: slot_of is a permutation of the storage rows. `windows`: within a row, the listed frames are stored on different indices of frames: the values slot_of[c] // 2 differ. `counts`: some query block has exactly 4 live entries.
All inputs are finite; a program needn't handle non-finite values.
Results may differ from a plain program's by a relative error of at most 0.01.
Values may be sent and summed in bfloat16 or wider, within the bound.
A program may use at most 64 MiB of HBM per device.

v0:
```python
import jax
import jax.numpy as jnp
from jax import lax
from jax.sharding import PartitionSpec as P


def attend(running, rows_q, key_rows, value_rows):
    old_top, denom_sum, weighted = running
    scores = jnp.einsum(
        "td,kd->tk", rows_q, key_rows, preferred_element_type=jnp.float32
    ) * rows_q.shape[1] ** (-0.5)
    new_top = jnp.maximum(old_top, jnp.max(scores, axis=1))
    raised = jnp.exp(scores - new_top[:, None])
    shrink = jnp.exp(old_top - new_top)
    denom_sum = denom_sum * shrink + jnp.sum(raised, axis=1)
    weighted = weighted * shrink[:, None] + jnp.dot(
        raised.astype(jnp.bfloat16), value_rows, preferred_element_type=jnp.float32
    )
    return (new_top, denom_sum, weighted)


def empty_state(row_count, width):
    return (
        jnp.full((row_count,), -jnp.inf, jnp.float32),
        jnp.zeros((row_count,), jnp.float32),
        jnp.zeros((row_count, width), jnp.float32),
    )


def listed_slots(windows, counts, slot_of):
    slot_total = slot_of.shape[0]
    frame_hit = windows[:, :, None] == jnp.arange(slot_total, dtype=jnp.int32)[None, None, :]
    slot_ids = jnp.sum(jnp.where(frame_hit, slot_of[None, None, :], 0), axis=2)
    in_use = jnp.arange(windows.shape[1], dtype=jnp.int32)[None, :] < counts[:, None]
    return (slot_ids, in_use)


def keep_state(state_in):
    return state_in


def local(
    queries,
    local_keys,
    local_values,
    cache_keys,
    cache_values,
    windows,
    counts,
    slot_of,
    residual,
    out_weight,
    gate_table,
    timestep,
):
    tok_rows, head_width = queries.shape
    slot_count = cache_keys.shape[0]
    my_block = lax.axis_index("frames")
    slot_ids, in_use = listed_slots(windows, counts, slot_of)
    own_state = attend(empty_state(tok_rows, head_width), queries, local_keys, local_values)
    my_slots = lax.dynamic_index_in_dim(slot_ids, my_block, 0, keepdims=False)
    my_use = lax.dynamic_index_in_dim(in_use, my_block, 0, keepdims=False)
    local_ids = my_block * slot_count + jnp.arange(slot_count, dtype=jnp.int32)
    wanted = jnp.any(
        (slot_ids[:, :, None] == local_ids[None, None, :]) & in_use[:, :, None], axis=1
    )
    chooser = wanted.astype(jnp.bfloat16)
    send_keys = jnp.einsum(
        "bk,kfc->bfc", chooser, cache_keys, preferred_element_type=jnp.float32
    ).astype(jnp.bfloat16)
    send_values = jnp.einsum(
        "bk,kfc->bfc", chooser, cache_values, preferred_element_type=jnp.float32
    ).astype(jnp.bfloat16)
    keys_in, values_in = (
        lax.all_to_all(send_keys, "frames", split_axis=0, concat_axis=0, tiled=True),
        lax.all_to_all(send_values, "frames", split_axis=0, concat_axis=0, tiled=True),
    )
    holder_range = jnp.arange(keys_in.shape[0], dtype=jnp.int32)
    live_from = jnp.any(
        ((my_slots // slot_count)[:, None] == holder_range[None, :]) & my_use[:, None], axis=0
    )

    def visit_holder(position, state_now):

        def take_holder(state_in):
            return attend(state_in, queries, keys_in[position], values_in[position])

        return lax.cond(live_from[position], take_holder, keep_state, state_now)

    row_top, denom_sum, weighted = lax.fori_loop(0, keys_in.shape[0], visit_holder, own_state)
    attended = (weighted / denom_sum[:, None]).astype(jnp.bfloat16)
    mixed = jnp.einsum(
        "dc,tc->dt",
        out_weight,
        lax.all_gather(attended, "heads", axis=1, tiled=True),
        preferred_element_type=jnp.float32,
    )
    picked = jnp.arange(gate_table.shape[0], dtype=jnp.int32) == timestep[0]
    gate_row = jnp.sum(jnp.where(picked[:, None], gate_table, 0.0), axis=0)
    return (residual.astype(jnp.float32) + gate_row[:, None] * mixed).astype(jnp.bfloat16)


def solution(mesh):
    return jax.shard_map(
        local,
        mesh=mesh,
        in_specs=(
            P("frames", "heads"),
            P("frames", "heads"),
            P("frames", "heads"),
            P("frames", None, "heads"),
            P("frames", None, "heads"),
            P(),
            P(),
            P(),
            P("heads", "frames"),
            P("heads", None),
            P(None, "heads"),
            P(),
        ),
        out_specs=P("heads", "frames"),
        check_vma=False,
    )
```

profile of v0, /device:TPU:2, one launch (start us, length us, event | category | flops | bytes accessed | tf_op | source)
XLA Modules:
  0.0 211.8 jit_solution(4480361472453399625)
XLA Ops:
  6.5 0.0 copy-start
  6.5 0.8 iota_compare_fusion.1
  7.4 0.1 copy.28
  7.5 0.9 select_reduce_fusion.1
  8.4 0.1 and_reduce_fusion
  8.5 1.8 convolution_convert_fusion.1
  10.2 1.9 copy.30
  12.1 9.4 %all-to-all-start = ((bf16[16,512,128]{2,1,0:T(8,128)(2,1)}), bf16[16,512,128]{2,1,0:T(8,128)(2,1)S(1)}, u32[]{:S(2)}, u32[]{:S(2)}) async-start(bf16[16,512,128]{2,1,0:T(8,128)(2,1)} %copy.30), calls=%async_computation | async-start | bytes 4194304 | tf_op jit(solution)/shard_map/all_to_all | solution.py:75
  21.5 1.7 convolution_convert_fusion
  23.3 1.8 copy.32
  25.1 23.8 %all-to-all-done = bf16[16,512,128]{2,1,0:T(8,128)(2,1)S(1)} async-done(((bf16[16,512,128]{2,1,0:T(8,128)(2,1)}), bf16[16,512,128]{2,1,0:T(8,128)(2,1)S(1)}, u32[]{:S(2)}, u32[]{:S(2)}) %all-to-all-start) | async-done | bytes 2097184 | tf_op jit(solution)/shard_map/all_to_all | solution.py:75
  48.9 6.8 %all-to-all-start.1 = ((bf16[16,512,128]{2,1,0:T(8,128)(2,1)}), bf16[16,512,128]{2,1,0:T(8,128)(2,1)}, u32[]{:S(2)}, u32[]{:S(2)}) async-start(bf16[16,512,128]{2,1,0:T(8,128)(2,1)} %copy.32), calls=%async_computation.1 | async-start | bytes 4194304 | tf_op jit(solution)/shard_map/all_to_all | solution.py:76
  55.7 0.0 all-gather.2.cloned.1.call-start
  55.7 0.2 dynamic-slice_reduce_fusion
  55.9 0.1 fusion.20
  56.0 0.0 copy-done.1
  56.0 0.0 copy-done.2
  56.0 0.2 fusion.25
  56.2 0.1 fusion.16
  56.3 1.1 convolution_add_fusion.1
  57.4 25.8 %all-to-all-done.1 = bf16[16,512,128]{2,1,0:T(8,128)(2,1)} async-done(((bf16[16,512,128]{2,1,0:T(8,128)(2,1)}), bf16[16,512,128]{2,1,0:T(8,128)(2,1)}, u32[]{:S(2)}, u32[]{:S(2)}) %all-to-all-start.1) | async-done | bytes 2097184 | tf_op jit(solution)/shard_map/all_to_all | solution.py:76
  83.2 22.6 %while.17 = (s32[]{:T(128)}, f32[256]{0:T(256)S(1)}, f32[256]{0:T(256)S(1)}, f32[256,128]{1,0:T(8,128)S(1)}, pred[16]{0:T(512)(128)(4,1)S(1)}, /*index=5*/bf16[1...) while((s32[]{:T(128)}, f32[256]{0:T(256)S(1)}, ...), condition=%wide.region_11.12_spmd, body=%wide.region_6.0_spmd.sunk | while | flops 67961344 | bytes 2179330 | solution.py:90
  83.2 0.6 dynamic_slice.36
  84.4 0.6 dynamic_slice.36
  85.7 0.6 dynamic_slice.36
  86.9 0.6 dynamic_slice.36
  88.2 0.6 dynamic_slice.36
  89.5 0.6 dynamic_slice.36
  90.7 0.6 dynamic_slice.36
  91.9 2.5 %conditional.2 = ((f32[256]{0:T(256)S(1)}, f32[256]{0:T(256)S(1)}, f32[256,128]{1,0:T(8,128)S(1)})) conditional(s32[]{:T(128)} %bitcast.30, (f32[256]{0:T(256)S(1)}, f32[256]{0:T(256)S(1)}, f32[256,128]{1,0:T(8,128)S(1)}) %tuple.42, (s32[]{:T(128)}, bf16[16,512,128]{2,1,0:T(8,128)(2,1)S(1)}, bf16[256,128]{1,0:T(8,128)(2,1)}, f32[256]{0:T(256)S(1)}, ...), branch_computations={%region_7.7_spmd, %region_8.10_spmd} | conditional | flops 67961344 | bytes 2179146 | solution.py:88
  92.0 1.1 fusion.24
  93.1 0.1 fusion.1
  93.2 1.2 convolution_add_fusion
  94.5 0.6 dynamic_slice.36
  95.7 0.6 dynamic_slice.36
  97.0 0.6 dynamic_slice.36
  98.2 0.6 dynamic_slice.36
  99.5 0.6 dynamic_slice.36
  100.7 0.6 dynamic_slice.36
  102.0 0.6 dynamic_slice.36
  103.2 0.6 dynamic_slice.36
  104.5 0.6 dynamic_slice.36
  105.7 0.7 divide_convert_fusion
  106.5 0.0 all-gather.2.cloned.1.call-update
  107.2 0.9 select_reduce_fusion
  108.1 93.8 %all-gather.2.cloned.1.call-done = bf16[256,4096]{1,0:T(8,128)(2,1)} async-done(((bf16[256,128]{1,0:T(8,128)(2,1)}), bf16[256,4096]{1,0:T(8,128)(2,1)}) %all-gather.2.cloned.1.call-update) | async-done | bytes 2097168 | tf_op jit(solution)/shard_map/all_gather | solution.py:95
  201.8 0.0 copy-done
  201.8 3.1 %fusion.12 = bf16[160,256]{1,0:T(8,128)(2,1)} fusion(bf16[256,4096]{1,0:T(8,128)(2,1)} %all-gather.2.cloned.1.call-done, bf16[160,4096]{1,0:T(8,128)(2,1)S(1)} %copy-done, bf16[160,256]{1,0:T(8,128)(2,1)} %param.24, f32[160]{0:T(256)S(1)} %select_reduce_fusion), kind=kOutput, calls=%fused_computation.21 | convolution fusion | flops 335708160 | bytes 3572352 | tf_op jit(solution)/shard_map/dc,tc->dt/dot_general | solution.py:92
  (25 shorter events, 0.2 us)
Async XLA Ops:
  6.5 195.3 %copy-start = (bf16[160,4096]{1,0:T(8,128)(2,1)S(1)}, bf16[160,4096]{1,0:T(8,128)(2,1)}, u32[]{:S(2)}) copy-start(bf16[160,4096]{1,0:T(8,128)(2,1)} %param.25) | copy-start | bytes 3932164
  12.1 36.8 %all-to-all-start = ((bf16[16,512,128]{2,1,0:T(8,128)(2,1)}), bf16[16,512,128]{2,1,0:T(8,128)(2,1)S(1)}, u32[]{:S(2)}, u32[]{:S(2)}) async-start(bf16[16,512,128]{2,1,0:T(8,128)(2,1)} %copy.30), calls=%async_computation | async-start | bytes 4194304 | tf_op jit(solution)/shard_map/all_to_all | solution.py:75
  25.1 30.9 %copy-start.1 = (bf16[256,128]{1,0:T(8,128)(2,1)S(1)}, bf16[256,128]{1,0:T(8,128)(2,1)}, u32[]{:S(2)}) copy-start(bf16[256,128]{1,0:T(8,128)(2,1)} %param.16) | copy-start | bytes 196612
  25.1 30.9 %copy-start.2 = (bf16[256,128]{1,0:T(8,128)(2,1)S(1)}, bf16[256,128]{1,0:T(8,128)(2,1)}, u32[]{:S(2)}) copy-start(bf16[256,128]{1,0:T(8,128)(2,1)} %param.17) | copy-start | bytes 196612
  48.9 34.3 %all-to-all-start.1 = ((bf16[16,512,128]{2,1,0:T(8,128)(2,1)}), bf16[16,512,128]{2,1,0:T(8,128)(2,1)}, u32[]{:S(2)}, u32[]{:S(2)}) async-start(bf16[16,512,128]{2,1,0:T(8,128)(2,1)} %copy.32), calls=%async_computation.1 | async-start | bytes 4194304 | tf_op jit(solution)/shard_map/all_to_all | solution.py:76
  55.7 146.2 %all-gather.2.cloned.1.call-start = ((), (), s32[]{:S(2)}) async-start(), calls=%async_computation.2 | async-start | bytes 2162688 | tf_op jit(solution)/shard_map/all_gather | solution.py:95
Sparse Core Ops, SparseCore 0:
  106.6 95.1 all-gather.1
where the time goes:
time: 215 us; the launch traced here: 212 us
  waiting for transfers between devices  143 us (67%)
  starting transfers between devices  16.2 us (8%)
  between operations  14.1 us (7%)
  local copies, waits for them, and re-layouts  13.6 us (6%)
  loops' own time  10.6 us (5%)
  matrix products  10.2 us (5%)
  other arithmetic  3.82 us (2%)
    all_gather x1, waiting for transfers between devices, local(): lax.all_gather(attended, 'heads', axis=1, tiled=True)  93.8 us
    all_to_all x1, waiting for transfers between devices, local(): lax.all_to_all(send_values, 'frames', split_axis=0, concat_axis=0, tiled=...  25.8 us
    all_to_all x1, waiting for transfers between devices, local(): lax.all_to_all(send_keys, 'frames', split_axis=0, concat_axis=0, tiled=True)  23.8 us
    another operation x1, loops' own time, local(): lax.fori_loop(0, keys_in.shape[0], visit_holder, own_state)  10.3 us
    dynamic_slice x16, local copies, waits for them, and re-layouts, visit_holder(): return lax.cond(live_from[position], take_holder, keep_state, state_now)  9.54 us
    all_to_all x1, starting transfers between devices, local(): lax.all_to_all(send_keys, 'frames', split_axis=0, concat_axis=0, tiled=True)  9.42 us
    all_to_all x1, starting transfers between devices, local(): lax.all_to_all(send_values, 'frames', split_axis=0, concat_axis=0, tiled=...  6.76 us
  transfers between devices with their start and end apart: 3, of which 3 were waited for; matrix products, arithmetic and copies ran while one was open for 3% of the time, Pallas kernels for 0%

commit v1 on v0

v1 whole, which is shorter than its diff:
```python
import functools

import jax
import jax.numpy as jnp
from jax import lax
from jax.experimental import pallas as pl
from jax.experimental.pallas import tpu as pltpu
from jax.sharding import PartitionSpec as P

MESH = pl.DeviceIdType.MESH
BF = jnp.bfloat16
F32 = jnp.float32
NX, NZL, NC, NZH, NY = 4, 2, 2, 4, 8
GROUP = NX * NZL
HEAD = 128
TOK = 256
FRAME = 512
FEAT = 160
HALF_FEAT = FEAT // 2
COLS = NY * HEAD
MSG = HEAD + 16
NEG = -(2.0**100)
SCALE2 = HEAD ** (-0.5) * 1.4426950408889634


def coords():
    f = lax.axis_index("frames")
    h = lax.axis_index("heads")
    return f // 8, (f // 2) % 4, f % 2, h // 8, h % 8


def device(zl, x, c, zh, y):
    return (zl * 8 + x * 2 + c, zh * 8 + y)


def kernel(
    splits,
    q_hbm, lk_hbm, lv_hbm, ck_hbm, cv_hbm, windows, counts, slot_of, res_hbm, w_hbm, gate_hbm, step,
    out_ref,
    qall, kbuf, vbuf, vt, lk, lv, lvt, sent, came, acc, top, den, att, wg, part, parts_in, resid, gate, gcol,
    sem_load, sem_kv_s, sem_kv_r, sem_q_s, sem_q_r, sem_p_s, sem_p_r,
    sem_a_s, sem_a_r, sem_w_s, sem_w_r, sem_f_s, sem_f_r, sem_m_s, sem_m_r,
):
    zl, x, c, zh, y = coords()
    width = TOK // splits

    def frame_peer(o, sign):
        dz, dx = o // NX, o % NX
        return device((zl + dz) % NZL, (x + sign * dx + NX) % NX, c, zh, y)

    def y_peer(k):
        return device(zl, x, c, zh, (y + k) % NY)

    def z_peer(k):
        return device(zl, x, c, (zh + k) % NZH, y)

    other_core = device(zl, x, 1 - c, zh, y)

    mine = pl.ds(pl.multiple_of(c * 2, 2), 2)
    loads = [
        pltpu.make_async_copy(ck_hbm, kbuf.at[mine], sem_load.at[0]),
        pltpu.make_async_copy(cv_hbm, vbuf.at[mine], sem_load.at[1]),
        pltpu.make_async_copy(q_hbm, qall.at[0], sem_load.at[2]),
        pltpu.make_async_copy(lk_hbm, lk, sem_load.at[3]),
        pltpu.make_async_copy(lv_hbm, lv, sem_load.at[4]),
        pltpu.make_async_copy(gate_hbm, gate, sem_load.at[5]),
        pltpu.make_async_copy(res_hbm, resid, sem_load.at[6]),
        pltpu.make_async_copy(
            w_hbm.at[:, pl.ds(pl.multiple_of(zh * COLS, COLS), COLS)], wg.at[zh], sem_load.at[7]
        ),
    ]
    for load in loads:
        load.start()

    barrier = pltpu.get_barrier_semaphore()
    peers = [other_core]
    peers += [frame_peer(o, 1) for o in range(1, GROUP)]
    peers += [y_peer(k) for k in range(1, NY)]
    peers += [z_peer(k) for k in range(1, NZH)]
    for peer in peers:
        pl.semaphore_signal(barrier, inc=1, device_id=peer, device_id_type=MESH)
    pl.semaphore_wait(barrier, len(peers))

    def remote(src, dst, send, recv, peer):
        return pltpu.make_async_remote_copy(
            src_ref=src, dst_ref=dst, send_sem=send, recv_sem=recv, device_id=peer, device_id_type=MESH
        )

    def span(t):
        return pl.ds(t * width, width)

    kv = [
        remote(ck_hbm, kbuf.at[mine], sem_kv_s.at[0], sem_kv_r.at[0], other_core),
        remote(cv_hbm, vbuf.at[mine], sem_kv_s.at[1], sem_kv_r.at[1], other_core),
    ]

    def q_copy(t, o):
        return remote(
            q_hbm.at[span(t)], qall.at[o, span(t)], sem_q_s.at[t, o], sem_q_r.at[t, o], frame_peer(o, 1)
        )

    def p_copy(t, o):
        return remote(sent.at[t, o], came.at[t, o], sem_p_s.at[t, o], sem_p_r.at[t, o], frame_peer(o, -1))

    def a_copy(t, k):
        return remote(att.at[t, y], att.at[t, y], sem_a_s.at[t, k], sem_a_r.at[t, k], y_peer(k))

    rows = pl.ds(pl.multiple_of(c * HALF_FEAT, 16), HALF_FEAT)

    def w_copy(k):
        there = (zh + k) % NZH
        return remote(
            w_hbm.at[rows, pl.ds(pl.multiple_of(there * COLS, COLS), COLS)],
            wg.at[zh, rows], sem_w_s.at[k], sem_w_r.at[k], z_peer(k),
        )

    def f_copy(k):
        there = (zh + NZH - k) % NZH
        return remote(wg.at[there, rows], wg.at[there, rows], sem_f_s.at[k], sem_f_r.at[k], other_core)

    def m_copy(t, k):
        return remote(part.at[t, k], parts_in.at[t, k], sem_m_s.at[t, k], sem_m_r.at[t, k], z_peer(k))

    for copy in kv:
        copy.start()
    for t in range(splits):

        @pl.loop(1, GROUP)
        def _(o):
            q_copy(t, o).start()

    for k in range(1, NZH):
        w_copy(k).start()

    for load in loads:
        load.wait()
    lvt[...] = lv[...].T
    for i in range(2):
        vt[c * 2 + i] = vbuf[c * 2 + i].T
    hot = lax.broadcasted_iota(jnp.int32, gate.shape, 0) == step[0]
    gcol[...] = jnp.sum(jnp.where(hot, gate[...], 0.0).T, axis=1, keepdims=True)
    for copy in kv:
        copy.wait_recv()
    for i in range(2):
        vt[(1 - c) * 2 + i] = vbuf[(1 - c) * 2 + i].T

    def listed(block, holder):
        frame, live = 0, 0
        for j in range(4):
            slot = slot_of[windows[block, j]]
            hit = jnp.logical_and(j < counts[block], slot // 2 == holder).astype(jnp.int32)
            frame = frame + hit * (slot % 2)
            live = live + hit
        return frame, live

    def scores(keys, q):
        return lax.dot_general(keys, q, (((1,), (1,)), ((), ())), preferred_element_type=F32)

    def attend(t, o, own):
        q = qall[o, span(t)]
        dz, dx = o // NX, o % NX
        block = ((zl + dz) % NZL) * 8 + ((x - dx + NX) % NX) * 2 + c
        pieces = []
        tops = []
        for d in range(2):
            frame, live = listed(block, zl * 8 + x * 2 + d)
            s = scores(kbuf[2 * d + frame], q) * SCALE2
            on = jnp.full((1, width), live, jnp.int32) > 0
            tops.append(jnp.where(on, jnp.max(s, axis=0, keepdims=True), NEG))
            pieces.append((s, on, vt[2 * d + frame]))
        if own:
            s = scores(lk[...], q) * SCALE2
            tops.append(jnp.max(s, axis=0, keepdims=True))
            pieces.append((s, None, lvt[...]))
        m = functools.reduce(jnp.maximum, tops).astype(BF).astype(F32)
        total, result = 0.0, 0.0
        for s, on, values in pieces:
            shift = -m if on is None else jnp.where(on, -m, NEG)
            p = jnp.exp2(s + shift)
            total = total + jnp.sum(p, axis=0, keepdims=True)
            result = result + jnp.dot(values, p.astype(BF), preferred_element_type=F32)
        return m, total, result

    def attend_own(t):
        m, total, result = attend(t, 0, True)
        acc[t] = result
        top[t] = jnp.broadcast_to(m, (8, width))
        den[t] = jnp.broadcast_to(total, (8, width))

    def visit(t, first, last):

        @pl.loop(first, last)
        def _(o):
            q_copy(t, o).wait_recv()
            m, total, result = attend(t, o, False)
            sent[t, o, 0:HEAD] = result.astype(BF)
            high = total.astype(BF).astype(F32)
            row = lax.broadcasted_iota(jnp.int32, (16, width), 0)
            stats = jnp.where(row == 0, m, jnp.where(row == 1, high, total - high))
            sent[t, o, HEAD:MSG] = stats.astype(BF)
            p_copy(t, o).start()

    def merge(t):

        @pl.loop(1, GROUP)
        def _(o):
            p_copy(t, o).wait_recv()
            stats = came[t, o, HEAD:MSG].astype(F32)
            m = stats[0:1]
            total = stats[1:2] + stats[2:3]
            old = top[t, 0:1]
            new = jnp.maximum(old, m)
            keep = jnp.exp2(old - new)
            take = jnp.exp2(m - new)
            acc[t] = acc[t] * keep + came[t, o, 0:HEAD].astype(F32) * take
            den[t] = jnp.broadcast_to(den[t, 0:1] * keep + total * take, (8, width))
            top[t] = jnp.broadcast_to(new, (8, width))

        att[t, y] = (acc[t] / den[t, 0:1]).astype(BF)

        @pl.loop(1, NY)
        def _(k):
            a_copy(t, k).start()

    def project(t):

        @pl.loop(1, NY)
        def _(k):
            a_copy(t, k).wait_recv()

        rows_in = att[t].reshape(COLS, width)

        @pl.loop(1, NZH)
        def _(k):
            mixed = jnp.dot(wg[(zh + k) % NZH], rows_in, preferred_element_type=F32)
            part[t, k] = mixed.astype(BF)
            m_copy(t, k).start()

        return jnp.dot(wg[zh], rows_in, preferred_element_type=F32)

    def finish(t, mixed):
        for k in range(1, NZH):
            m_copy(t, k).wait_recv()
            mixed = mixed + parts_in[t, k].astype(F32)
        out_ref[:, span(t)] = (resid[:, span(t)].astype(F32) + gcol[...] * mixed).astype(BF)

    attend_own(0)
    visit(0, 1, GROUP)
    for t in range(1, splits):
        attend_own(t)
        visit(t, 1, GROUP // 2)
        merge(t - 1)
        visit(t, GROUP // 2, GROUP)
    merge(splits - 1)
    for k in range(1, NZH):
        w_copy(k).wait_recv()
        f_copy(k).start()
    for k in range(1, NZH):
        f_copy(k).wait_recv()
    own_parts = [project(t) for t in range(splits)]
    for t in range(splits):
        finish(t, own_parts[t])

    for copy in kv:
        copy.wait_send()
    for t in range(splits):

        @pl.loop(1, GROUP)
        def _(o):
            q_copy(t, o).wait_send()
            p_copy(t, o).wait_send()

        @pl.loop(1, NY)
        def _(k):
            a_copy(t, k).wait_send()

        for k in range(1, NZH):
            m_copy(t, k).wait_send()
    for k in range(1, NZH):
        w_copy(k).wait_send()
        f_copy(k).wait_send()


def local(splits, *args):
    width = TOK // splits
    anywhere = pl.BlockSpec(memory_space=pl.ANY)
    smem = pl.BlockSpec(memory_space=pltpu.SMEM)
    dma = pltpu.SemaphoreType.DMA
    return pl.pallas_call(
        functools.partial(kernel, splits),
        out_shape=jax.ShapeDtypeStruct((FEAT, TOK), BF),
        in_specs=[anywhere] * 5 + [smem] * 3 + [anywhere] * 3 + [smem],
        out_specs=pl.BlockSpec(memory_space=pltpu.VMEM),
        scratch_shapes=[
            pltpu.VMEM((GROUP, TOK, HEAD), BF),
            pltpu.VMEM((4, FRAME, HEAD), BF),
            pltpu.VMEM((4, FRAME, HEAD), BF),
            pltpu.VMEM((4, HEAD, FRAME), BF),
            pltpu.VMEM((TOK, HEAD), BF),
            pltpu.VMEM((TOK, HEAD), BF),
            pltpu.VMEM((HEAD, TOK), BF),
            pltpu.VMEM((splits, GROUP, MSG, width), BF),
            pltpu.VMEM((splits, GROUP, MSG, width), BF),
            pltpu.VMEM((splits, HEAD, width), F32),
            pltpu.VMEM((splits, 8, width), F32),
            pltpu.VMEM((splits, 8, width), F32),
            pltpu.VMEM((splits, NY, HEAD, width), BF),
            pltpu.VMEM((NZH, FEAT, COLS), BF),
            pltpu.VMEM((splits, NZH, FEAT, width), BF),
            pltpu.VMEM((splits, NZH, FEAT, width), BF),
            pltpu.VMEM((FEAT, TOK), BF),
            pltpu.VMEM((50, FEAT), F32),
            pltpu.VMEM((FEAT, 1), F32),
            dma((8,)),
            dma((2,)), dma((2,)),
            dma((splits, GROUP)), dma((splits, GROUP)),
            dma((splits, GROUP)), dma((splits, GROUP)),
            dma((splits, NY)), dma((splits, NY)),
            dma((NZH,)), dma((NZH,)),
            dma((NZH,)), dma((NZH,)),
            dma((splits, NZH)), dma((splits, NZH)),
        ],
        compiler_params=pltpu.CompilerParams(
            collective_id=0, has_side_effects=True, vmem_limit_bytes=32 << 20
        ),
        name="block_attention_projection",
    )(*args)


def solution(mesh):
    return jax.shard_map(
        functools.partial(local, 1),
        mesh=mesh,
        in_specs=(
            P("frames", "heads"),
            P("frames", "heads"),
            P("frames", "heads"),
            P("frames", None, "heads"),
            P("frames", None, "heads"),
            P(),
            P(),
            P(),
            P("heads", "frames"),
            P("heads", None),
            P(None, "heads"),
            P(),
        ),
        out_specs=P("heads", "frames"),
        check_vma=False,
    )
```

time: 215 us -> 78.5 us (0.37)
  the two profiles are of different devices: /device:TPU:2 before, /device:TPU:17 now
where the time goes in v1:
time: 78.5 us; the launch traced here: 78 us
  Pallas kernels  67.2 us (86%)
  local copies, waits for them, and re-layouts  10.1 us (13%)
    pallas_call x1, Pallas kernels, local(): pl.pallas_call(functools.partial(kernel, splits), out_shape=jax.ShapeDtyp...  67.2 us
    unnamed x22, local copies, waits for them, and re-layouts  10.1 us

profile of v1, /device:TPU:17, one launch (start us, length us, event | category | flops | bytes accessed | tf_op | source)
XLA Modules:
  0.0 78.0 jit_solution(10902856219218485976)
XLA Ops:
  0.7 0.8 copy.13.windows
  1.4 0.0 copy-start
  1.4 1.3 %copy-done = bf16[160,4096]{1,0:T(8,128)(2,1)S(1)} copy-done((bf16[160,4096]{1,0:T(8,128)(2,1)S(1)}, bf16[160,4096]{1,0:T(8,128)(2,1)}, u32[]{:S(2)}) %copy-start) | copy-done | bytes 1310744
  2.7 0.0 copy-start.1
  2.7 0.9 %copy-done.1 = bf16[2,512,128]{2,1,0:T(8,128)(2,1)S(1)} copy-done((bf16[2,512,128]{2,1,0:T(8,128)(2,1)S(1)}, bf16[2,512,128]{2,1,0:T(8,128)(2,1)}, u32[]{:S(2)}) %copy-start.1) | copy-done | bytes 262168
  3.7 0.0 copy-start.2
  3.7 0.9 %copy-done.2 = bf16[2,512,128]{2,1,0:T(8,128)(2,1)S(1)} copy-done((bf16[2,512,128]{2,1,0:T(8,128)(2,1)S(1)}, bf16[2,512,128]{2,1,0:T(8,128)(2,1)}, u32[]{:S(2)}) %copy-start.2) | copy-done | bytes 262168
  4.6 0.0 copy-start.3
  4.6 0.9 %copy-done.3 = bf16[160,256]{1,0:T(8,128)(2,1)S(1)} copy-done((bf16[160,256]{1,0:T(8,128)(2,1)S(1)}, bf16[160,256]{1,0:T(8,128)(2,1)}, u32[]{:S(2)}) %copy-start.3) | copy-done | bytes 81944
  5.5 0.0 copy-start.4
  5.5 0.8 %copy-done.4 = bf16[256,128]{1,0:T(8,128)(2,1)S(1)} copy-done((bf16[256,128]{1,0:T(8,128)(2,1)S(1)}, bf16[256,128]{1,0:T(8,128)(2,1)}, u32[]{:S(2)}) %copy-start.4) | copy-done | bytes 65560
  6.4 0.0 copy-start.5
  6.4 0.8 %copy-done.5 = bf16[256,128]{1,0:T(8,128)(2,1)S(1)} copy-done((bf16[256,128]{1,0:T(8,128)(2,1)S(1)}, bf16[256,128]{1,0:T(8,128)(2,1)}, u32[]{:S(2)}) %copy-start.5) | copy-done | bytes 65560
  7.2 0.0 copy-start.6
  7.2 0.8 %copy-done.6 = bf16[256,128]{1,0:T(8,128)(2,1)S(1)} copy-done((bf16[256,128]{1,0:T(8,128)(2,1)S(1)}, bf16[256,128]{1,0:T(8,128)(2,1)}, u32[]{:S(2)}) %copy-start.6) | copy-done | bytes 65560
  8.0 0.0 copy-start.7
  8.0 0.8 %copy-done.7 = f32[50,160]{1,0:T(8,128)S(1)} copy-done((f32[50,160]{1,0:T(8,128)S(1)}, f32[50,160]{1,0:T(8,128)}, u32[]{:S(2)}) %copy-start.7) | copy-done | bytes 32024
  8.9 0.0 copy-start.8
  8.9 0.7 copy-done.8
  9.5 0.0 copy-start.9
  9.5 0.7 copy-done.9
  10.2 67.2 %block_attention_projection.1 = bf16[160,256]{1,0:T(8,128)(2,1)S(1)} custom-call(bf16[256,128]{1,0:T(8,128)(2,1)S(1)} %copy-done.4, bf16[256,128]{1,0:T(8,128)(2,1)S(1)} %copy-done.5, bf16[256,128]{1,0:T(8,128)(2,1)S(1)} %copy-done.6, bf16[2,512,128]{2,1,0:T(8,128)(2,1)S(1)} %copy-done.1, bf16[2,512,128]{2,1,0:T(8,128)(2,1)S(1)} %copy-done.2, ...), custom_call_target="tpu_custom_call" | custom-call | tf_op jit(solution)/shard_map/block_attention_projection/pallas_call | solution.py:289
  77.4 0.6 copy.16
Async XLA Ops:
  1.4 1.3 %copy-start = (bf16[160,4096]{1,0:T(8,128)(2,1)S(1)}, bf16[160,4096]{1,0:T(8,128)(2,1)}, u32[]{:S(2)}) copy-start(bf16[160,4096]{1,0:T(8,128)(2,1)} %w_hbm.1) | copy-start | bytes 3932164
  2.7 0.9 %copy-start.1 = (bf16[2,512,128]{2,1,0:T(8,128)(2,1)S(1)}, bf16[2,512,128]{2,1,0:T(8,128)(2,1)}, u32[]{:S(2)}) copy-start(bf16[2,512,128]{2,1,0:T(8,128)(2,1)} %ck_hbm.1) | copy-start | bytes 786436
  3.7 0.9 %copy-start.2 = (bf16[2,512,128]{2,1,0:T(8,128)(2,1)S(1)}, bf16[2,512,128]{2,1,0:T(8,128)(2,1)}, u32[]{:S(2)}) copy-start(bf16[2,512,128]{2,1,0:T(8,128)(2,1)} %cv_hbm.1) | copy-start | bytes 786436
  4.6 0.9 %copy-start.3 = (bf16[160,256]{1,0:T(8,128)(2,1)S(1)}, bf16[160,256]{1,0:T(8,128)(2,1)}, u32[]{:S(2)}) copy-start(bf16[160,256]{1,0:T(8,128)(2,1)} %res_hbm.1) | copy-start | bytes 245764
  5.5 0.8 %copy-start.4 = (bf16[256,128]{1,0:T(8,128)(2,1)S(1)}, bf16[256,128]{1,0:T(8,128)(2,1)}, u32[]{:S(2)}) copy-start(bf16[256,128]{1,0:T(8,128)(2,1)} %q_hbm.1) | copy-start | bytes 196612
  6.4 0.8 %copy-start.5 = (bf16[256,128]{1,0:T(8,128)(2,1)S(1)}, bf16[256,128]{1,0:T(8,128)(2,1)}, u32[]{:S(2)}) copy-start(bf16[256,128]{1,0:T(8,128)(2,1)} %lk_hbm.1) | copy-start | bytes 196612
  7.2 0.8 %copy-start.6 = (bf16[256,128]{1,0:T(8,128)(2,1)S(1)}, bf16[256,128]{1,0:T(8,128)(2,1)}, u32[]{:S(2)}) copy-start(bf16[256,128]{1,0:T(8,128)(2,1)} %lv_hbm.1) | copy-start | bytes 196612
  8.0 0.8 %copy-start.7 = (f32[50,160]{1,0:T(8,128)S(1)}, f32[50,160]{1,0:T(8,128)}, u32[]{:S(2)}) copy-start(f32[50,160]{1,0:T(8,128)} %gate_hbm.1) | copy-start | bytes 96004
  8.9 0.7 copy-start.8
  9.5 0.7 copy-start.9

commit v2 on v1

--- a/solution.py
+++ b/solution.py
@@ -17,7 +17,7 @@
 FRAME = 512
 FEAT = 160
 HALF_FEAT = FEAT // 2
-COLS = NY * HEAD
+COLS = 8 * HEAD
 MSG = HEAD + 16
 NEG = -(2.0**100)
 SCALE2 = HEAD ** (-0.5) * 1.4426950408889634
@@ -48,11 +48,13 @@
         dz, dx = o // NX, o % NX
         return device((zl + dz) % NZL, (x + sign * dx + NX) % NX, c, zh, y)
 
-    def y_peer(k):
-        return device(zl, x, c, zh, (y + k) % NY)
-
-    def z_peer(k):
-        return device(zl, x, c, (zh + k) % NZH, y)
+    pair, side = y // 2, y % 2
+
+    def set_peer(k):
+        return device(zl, x, c, (zh + k // 2) % NZH, 2 * pair + (side + k) % 2)
+
+    def feature_peer(k):
+        return device(zl, x, c, zh, (y + 2 * k) % NY)
 
     other_core = device(zl, x, 1 - c, zh, y)
 
@@ -65,18 +67,22 @@
         pltpu.make_async_copy(lv_hbm, lv, sem_load.at[4]),
         pltpu.make_async_copy(gate_hbm, gate, sem_load.at[5]),
         pltpu.make_async_copy(res_hbm, resid, sem_load.at[6]),
-        pltpu.make_async_copy(
-            w_hbm.at[:, pl.ds(pl.multiple_of(zh * COLS, COLS), COLS)], wg.at[zh], sem_load.at[7]
-        ),
     ]
+    for z in range(NZH):
+        loads.append(
+            pltpu.make_async_copy(
+                w_hbm.at[:, pl.ds(pl.multiple_of(z * 1024 + pair * 256, 256), 256)],
+                wg.at[pair, :, pl.ds(z * 256, 256)], sem_load.at[7 + z],
+            )
+        )
     for load in loads:
         load.start()
 
     barrier = pltpu.get_barrier_semaphore()
     peers = [other_core]
     peers += [frame_peer(o, 1) for o in range(1, GROUP)]
-    peers += [y_peer(k) for k in range(1, NY)]
-    peers += [z_peer(k) for k in range(1, NZH)]
+    peers += [set_peer(k) for k in range(1, 8)]
+    peers += [feature_peer(k) for k in range(1, 4)]
     for peer in peers:
         pl.semaphore_signal(barrier, inc=1, device_id=peer, device_id_type=MESH)
     pl.semaphore_wait(barrier, len(peers))
@@ -103,23 +109,24 @@
         return remote(sent.at[t, o], came.at[t, o], sem_p_s.at[t, o], sem_p_r.at[t, o], frame_peer(o, -1))
 
     def a_copy(t, k):
-        return remote(att.at[t, y], att.at[t, y], sem_a_s.at[t, k], sem_a_r.at[t, k], y_peer(k))
+        here = att.at[t, 2 * zh + side]
+        return remote(here, here, sem_a_s.at[t, k], sem_a_r.at[t, k], set_peer(k))
 
     rows = pl.ds(pl.multiple_of(c * HALF_FEAT, 16), HALF_FEAT)
 
-    def w_copy(k):
-        there = (zh + k) % NZH
+    def w_copy(k, z):
+        there = (pair + k) % 4
         return remote(
-            w_hbm.at[rows, pl.ds(pl.multiple_of(there * COLS, COLS), COLS)],
-            wg.at[zh, rows], sem_w_s.at[k], sem_w_r.at[k], z_peer(k),
+            w_hbm.at[rows, pl.ds(pl.multiple_of(z * 1024 + there * 256, 256), 256)],
+            wg.at[pair, rows, pl.ds(z * 256, 256)], sem_w_s.at[k, z], sem_w_r.at[k, z], feature_peer(k),
         )
 
     def f_copy(k):
-        there = (zh + NZH - k) % NZH
-        return remote(wg.at[there, rows], wg.at[there, rows], sem_f_s.at[k], sem_f_r.at[k], other_core)
+        block = wg.at[(pair + 4 - k) % 4, rows]
+        return remote(block, block, sem_f_s.at[k], sem_f_r.at[k], other_core)
 
     def m_copy(t, k):
-        return remote(part.at[t, k], parts_in.at[t, k], sem_m_s.at[t, k], sem_m_r.at[t, k], z_peer(k))
+        return remote(part.at[t, k], parts_in.at[t, k], sem_m_s.at[t, k], sem_m_r.at[t, k], feature_peer(k))
 
     for copy in kv:
         copy.start()
@@ -129,8 +136,9 @@
         def _(o):
             q_copy(t, o).start()
 
-    for k in range(1, NZH):
-        w_copy(k).start()
+    for k in range(1, 4):
+        for z in range(NZH):
+            w_copy(k, z).start()
 
     for load in loads:
         load.wait()
@@ -216,30 +224,30 @@
             den[t] = jnp.broadcast_to(den[t, 0:1] * keep + total * take, (8, width))
             top[t] = jnp.broadcast_to(new, (8, width))
 
-        att[t, y] = (acc[t] / den[t, 0:1]).astype(BF)
-
-        @pl.loop(1, NY)
+        att[t, 2 * zh + side] = (acc[t] / den[t, 0:1]).astype(BF)
+
+        @pl.loop(1, 8)
         def _(k):
             a_copy(t, k).start()
 
     def project(t):
 
-        @pl.loop(1, NY)
+        @pl.loop(1, 8)
         def _(k):
             a_copy(t, k).wait_recv()
 
         rows_in = att[t].reshape(COLS, width)
 
-        @pl.loop(1, NZH)
+        @pl.loop(1, 4)
         def _(k):
-            mixed = jnp.dot(wg[(zh + k) % NZH], rows_in, preferred_element_type=F32)
+            mixed = jnp.dot(wg[(pair + k) % 4], rows_in, preferred_element_type=F32)
             part[t, k] = mixed.astype(BF)
             m_copy(t, k).start()
 
-        return jnp.dot(wg[zh], rows_in, preferred_element_type=F32)
+        return jnp.dot(wg[pair], rows_in, preferred_element_type=F32)
 
     def finish(t, mixed):
-        for k in range(1, NZH):
+        for k in range(1, 4):
             m_copy(t, k).wait_recv()
             mixed = mixed + parts_in[t, k].astype(F32)
         out_ref[:, span(t)] = (resid[:, span(t)].astype(F32) + gcol[...] * mixed).astype(BF)
@@ -252,10 +260,11 @@
         merge(t - 1)
         visit(t, GROUP // 2, GROUP)
     merge(splits - 1)
-    for k in range(1, NZH):
-        w_copy(k).wait_recv()
+    for k in range(1, 4):
+        for z in range(NZH):
+            w_copy(k, z).wait_recv()
         f_copy(k).start()
-    for k in range(1, NZH):
+    for k in range(1, 4):
         f_copy(k).wait_recv()
     own_parts = [project(t) for t in range(splits)]
     for t in range(splits):
@@ -270,14 +279,15 @@
             q_copy(t, o).wait_send()
             p_copy(t, o).wait_send()
 
-        @pl.loop(1, NY)
+        @pl.loop(1, 8)
         def _(k):
             a_copy(t, k).wait_send()
 
-        for k in range(1, NZH):
+        for k in range(1, 4):
             m_copy(t, k).wait_send()
-    for k in range(1, NZH):
-        w_copy(k).wait_send()
+    for k in range(1, 4):
+        for z in range(NZH):
+            w_copy(k, z).wait_send()
         f_copy(k).wait_send()
 
 
@@ -304,24 +314,24 @@
             pltpu.VMEM((splits, HEAD, width), F32),
             pltpu.VMEM((splits, 8, width), F32),
             pltpu.VMEM((splits, 8, width), F32),
-            pltpu.VMEM((splits, NY, HEAD, width), BF),
+            pltpu.VMEM((splits, 8, HEAD, width), BF),
             pltpu.VMEM((NZH, FEAT, COLS), BF),
             pltpu.VMEM((splits, NZH, FEAT, width), BF),
             pltpu.VMEM((splits, NZH, FEAT, width), BF),
             pltpu.VMEM((FEAT, TOK), BF),
             pltpu.VMEM((50, FEAT), F32),
             pltpu.VMEM((FEAT, 1), F32),
-            dma((8,)),
+            dma((11,)),
             dma((2,)), dma((2,)),
             dma((splits, GROUP)), dma((splits, GROUP)),
             dma((splits, GROUP)), dma((splits, GROUP)),
             dma((splits, NY)), dma((splits, NY)),
-            dma((NZH,)), dma((NZH,)),
-            dma((NZH,)), dma((NZH,)),
+            dma((4, NZH)), dma((4, NZH)),
+            dma((4,)), dma((4,)),
             dma((splits, NZH)), dma((splits, NZH)),
         ],
         compiler_params=pltpu.CompilerParams(
-            collective_id=0, has_side_effects=True, vmem_limit_bytes=32 << 20
+            collective_id=0, has_side_effects=True, vmem_limit_bytes=60 << 20
         ),
         name="block_attention_projection",
     )(*args)

time: 78.5 us -> 66.4 us (0.85)
  the two profiles are of different devices: /device:TPU:17 before, /device:TPU:2 now
where the time goes in v2:
time: 66.4 us; the launch traced here: 66.2 us
  Pallas kernels  62.7 us (94%)
  local copies, waits for them, and re-layouts  2.88 us (4%)
    pallas_call x1, Pallas kernels, local(): pl.pallas_call(functools.partial(kernel, splits), out_shape=jax.ShapeDtyp...  62.7 us
    unnamed x2, local copies, waits for them, and re-layouts  2.88 us

profile of v2, /device:TPU:2, one launch (start us, length us, event | category | flops | bytes accessed | tf_op | source)
XLA Modules:
  0.0 66.2 jit_solution(8536268799612064082)
XLA Ops:
  0.7 1.4 %copy.13.windows = s32[16,4]{1,0:T(8,128)} copy(s32[16,4]{0,1:T(4,128)} %param.17) | data formatting | bytes 512 | tf_op args[5]
  2.0 62.7 %block_attention_projection.1 = bf16[160,256]{1,0:T(8,128)(2,1)} custom-call(bf16[256,128]{1,0:T(8,128)(2,1)} %q_hbm.1, bf16[256,128]{1,0:T(8,128)(2,1)} %lk_hbm.1, bf16[256,128]{1,0:T(8,128)(2,1)} %lv_hbm.1, bf16[2,512,128]{2,1,0:T(8,128)(2,1)} %ck_hbm.1, bf16[2,512,128]{2,1,0:T(8,128)(2,1)} %cv_hbm.1, s32[16,4]{1,0:T(8,128)} %copy.13.windows, s32[16]{0:T(128)} %counts.1, ...), custom_call_target="tpu_custom_call" | custom-call | tf_op jit(solution)/shard_map/block_attention_projection/pallas_call | solution.py:299
  64.7 1.5 %copy.16 = bf16[160,256]{1,0:T(8,128)(2,1)} copy(bf16[160,256]{1,0:T(8,128)(2,1)} %block_attention_projection.1) | data formatting | bytes 163840

commit v3 on v2

v3 whole, which is shorter than its diff:
```python
import functools

import jax
import jax.numpy as jnp
from jax import lax
from jax.experimental import pallas as pl
from jax.experimental.pallas import tpu as pltpu
from jax.sharding import PartitionSpec as P

MESH = pl.DeviceIdType.MESH
BF = jnp.bfloat16
F32 = jnp.float32
NX, NZL, NC, NZH, NY = 4, 2, 2, 4, 8
GROUP = NX * NZL
HEAD = 128
TOK = 256
FRAME = 512
FEAT = 160
HALF_FEAT = FEAT // 2
COLS = 8 * HEAD
MSG = HEAD + 16
NEG = -(2.0**100)
SCALE2 = HEAD ** (-0.5) * 1.4426950408889634


def coords():
    f = lax.axis_index("frames")
    h = lax.axis_index("heads")
    return f // 8, (f // 2) % 4, f % 2, h // 8, h % 8


def device(zl, x, c, zh, y):
    return (zl * 8 + x * 2 + c, zh * 8 + y)


def kernel(
    splits,
    q_hbm, lk_hbm, lv_hbm, ck_hbm, cv_hbm, windows_hbm, counts_hbm, slots_hbm, res_hbm, w_hbm, gate_hbm, step_hbm,
    out_ref,
    qall, kbuf, vbuf, vt, lk, lv, lvt, sent, came, att, wg, part, parts_in, resid, gate, gcol,
    windows, counts, slot_of, step,
    sem_load, sem_kv_s, sem_kv_r, sem_q_s, sem_q_r, sem_p_s, sem_p_r,
    sem_a_s, sem_a_r, sem_w_s, sem_w_r, sem_f_s, sem_f_r, sem_m_s, sem_m_r,
):
    zl, x, c, zh, y = coords()
    width = TOK // splits
    pair, side = y // 2, y % 2

    def frame_peer(o, sign):
        dz, dx = o // NX, o % NX
        return device((zl + dz) % NZL, (x + sign * dx + NX) % NX, c, zh, y)

    def z_peer(k):
        return device(zl, x, c, (zh + k) % NZH, y)

    def feature_peer(k):
        return device(zl, x, c, zh, (y + 2 * k) % NY)

    other_core = device(zl, x, 1 - c, zh, y)
    other_side = device(zl, x, c, zh, 2 * pair + 1 - side)

    mine = pl.ds(pl.multiple_of(c * 2, 2), 2)
    near = [
        (ck_hbm, kbuf.at[mine]), (cv_hbm, vbuf.at[mine]), (q_hbm, qall.at[0]), (lk_hbm, lk), (lv_hbm, lv),
        (windows_hbm, windows), (counts_hbm, counts), (slots_hbm, slot_of), (step_hbm, step), (gate_hbm, gate),
        (res_hbm, resid),
    ]
    for z in range(NZH):
        near.append((
            w_hbm.at[:, pl.ds(pl.multiple_of(z * 1024 + pair * 256, 256), 256)],
            wg.at[pair, :, pl.ds(z * 256, 256)],
        ))
    loads = [pltpu.make_async_copy(src, dst, sem_load.at[i]) for i, (src, dst) in enumerate(near)]
    for load in loads:
        load.start()

    barrier = pltpu.get_barrier_semaphore()
    peers = [other_core, other_side]
    peers += [frame_peer(o, 1) for o in range(1, GROUP)]
    peers += [z_peer(k) for k in range(1, NZH)]
    peers += [feature_peer(k) for k in range(1, 4)]
    for peer in peers:
        pl.semaphore_signal(barrier, inc=1, device_id=peer, device_id_type=MESH)
    pl.semaphore_wait(barrier, len(peers))

    def remote(src, dst, send, recv, peer):
        return pltpu.make_async_remote_copy(
            src_ref=src, dst_ref=dst, send_sem=send, recv_sem=recv, device_id=peer, device_id_type=MESH
        )

    def span(t):
        return pl.ds(t * width, width)

    kv = [
        remote(ck_hbm, kbuf.at[mine], sem_kv_s.at[0], sem_kv_r.at[0], other_core),
        remote(cv_hbm, vbuf.at[mine], sem_kv_s.at[1], sem_kv_r.at[1], other_core),
    ]

    def q_copy(t, o):
        return remote(
            q_hbm.at[span(t)], qall.at[o, span(t)], sem_q_s.at[t, o], sem_q_r.at[t, o], frame_peer(o, 1)
        )

    def p_copy(t, o):
        return remote(sent.at[t, o], came.at[t, o], sem_p_s.at[t, o], sem_p_r.at[t, o], frame_peer(o, -1))

    def a_copy(t, k):
        here = att.at[t, 2 * ((zh + (0 if k < 4 else 8 - k)) % NZH) + side]
        peer = z_peer(k) if 0 < k < 4 else other_side
        return remote(here, here, sem_a_s.at[t, k], sem_a_r.at[t, k], peer)

    rows = pl.ds(pl.multiple_of(c * HALF_FEAT, 16), HALF_FEAT)

    def w_copy(k, z):
        there = (pair + k) % 4
        return remote(
            w_hbm.at[rows, pl.ds(pl.multiple_of(z * 1024 + there * 256, 256), 256)],
            wg.at[pair, rows, pl.ds(z * 256, 256)], sem_w_s.at[k, z], sem_w_r.at[k, z], feature_peer(k),
        )

    def f_copy(k):
        block = wg.at[(pair + 4 - k) % 4, rows]
        return remote(block, block, sem_f_s.at[k], sem_f_r.at[k], other_core)

    def m_copy(t, k):
        return remote(part.at[t, k], parts_in.at[t, k], sem_m_s.at[t, k], sem_m_r.at[t, k], feature_peer(k))

    q_order = [1, 4, 3, 2, 5, 7, 6]
    for copy in kv:
        copy.start()
    for t in range(splits):
        for o in q_order:
            q_copy(t, o).start()
    if W_ON:
        for k in (2, 1, 3):
            for z in range(NZH):
                w_copy(k, z).start()

    for load in loads:
        load.wait()
    lvt[...] = lv[...].T
    for i in range(2):
        vt[c * 2 + i] = vbuf[c * 2 + i].T
    hot = lax.broadcasted_iota(jnp.int32, gate.shape, 0) == step[0]
    gcol[...] = jnp.sum(jnp.where(hot, gate[...], 0.0).T, axis=1, keepdims=True)
    for copy in kv:
        copy.wait_recv()
    for i in range(2):
        vt[(1 - c) * 2 + i] = vbuf[(1 - c) * 2 + i].T

    def listed(block, holder):
        frame, live = 0, 0
        for j in range(4):
            slot = slot_of[windows[j, block]]
            hit = jnp.logical_and(j < counts[block], slot // 2 == holder).astype(jnp.int32)
            frame = frame + hit * (slot % 2)
            live = live + hit
        return frame, live

    def scores(keys, q):
        return lax.dot_general(keys, q, (((1,), (1,)), ((), ())), preferred_element_type=F32)

    def attend(t, offsets):
        units = []
        for o in offsets:
            q = qall[o, span(t)]
            dz, dx = o // NX, o % NX
            block = ((zl + dz) % NZL) * 8 + ((x - dx + NX) % NX) * 2 + c
            pieces = []
            for d in range(2):
                frame, live = listed(block, zl * 8 + x * 2 + d)
                pieces.append((scores(kbuf[2 * d + frame], q), jnp.full((1, width), live, jnp.int32) > 0, vt.at[2 * d + frame]))
            if o == 0:
                pieces.append((scores(lk[...], q), None, lvt))
            units.append(pieces)
        results = []
        for pieces in units:
            tops = []
            for s, on, _ in pieces:
                top = jnp.max(s, axis=0, keepdims=True) * SCALE2
                tops.append(top if on is None else jnp.where(on, top, NEG))
            m = functools.reduce(jnp.maximum, tops).astype(BF).astype(F32)
            total, result = 0.0, 0.0
            for s, on, values in pieces:
                p = jnp.exp2(s * SCALE2 + (-m if on is None else jnp.where(on, -m, NEG)))
                total = total + jnp.sum(p, axis=0, keepdims=True)
                result = result + jnp.dot(values[...], p.astype(BF), preferred_element_type=F32)
            results.append((m, total, result))
        return results

    def visit(t, offsets):
        for o in offsets:
            if o > 0:
                q_copy(t, o).wait_recv()
        for o, (m, total, result) in zip(offsets, attend(t, offsets)):
            high = total.astype(BF).astype(F32)
            row = lax.broadcasted_iota(jnp.int32, (16, width), 0)
            stats = jnp.where(row == 0, m, jnp.where(row == 1, high, total - high))
            sent[t, o, 0:HEAD] = result.astype(BF)
            sent[t, o, HEAD:MSG] = stats.astype(BF)
            if o > 0:
                p_copy(t, o).start()

    def merge(t):
        for o in range(1, GROUP):
            p_copy(t, o).wait_recv()
        stats = [(sent if o == 0 else came)[t, o, HEAD:MSG].astype(F32) for o in range(GROUP)]
        m = functools.reduce(jnp.maximum, [each[0:1] for each in stats])
        total, result = 0.0, 0.0
        for o in range(GROUP):
            share = jnp.exp2(stats[o][0:1] - m)
            total = total + share * (stats[o][1:2] + stats[o][2:3])
            result = result + share * (sent if o == 0 else came)[t, o, 0:HEAD].astype(F32)
        att[t, 2 * zh + side] = (result / total).astype(BF)
        for k in (2, 1, 3, 0):
            a_copy(t, k).start()

    def spread(t):
        for k in (1, 3, 2):
            a_copy(t, k).wait_recv()
            a_copy(t, 4 + k).start()

    def project(t):
        for k in (0, 5, 7, 6):
            a_copy(t, k).wait_recv()
        rows_in = att[t].reshape(COLS, width)
        for k in (2, 1, 3):
            mixed = jnp.dot(wg[(pair + k) % 4], rows_in, preferred_element_type=F32)
            part[t, k] = mixed.astype(BF)
            m_copy(t, k).start()
        return jnp.dot(wg[pair], rows_in, preferred_element_type=F32)

    def finish(t, mixed):
        for k in (1, 3, 2):
            m_copy(t, k).wait_recv()
            mixed = mixed + parts_in[t, k].astype(F32)
        out_ref[:, span(t)] = (resid[:, span(t)].astype(F32) + gcol[...] * mixed).astype(BF)

    def forward_weights():
        for k in (1, 3, 2):
            for z in range(NZH):
                w_copy(k, z).wait_recv()
            f_copy(k).start()

    first, second = [0, 1, 4, 3], [2, 5, 7, 6]
    visit(0, first)
    visit(0, second)
    if splits == 2:
        visit(1, first)
        merge(0)
        visit(1, second)
        spread(0)
    merge(splits - 1)
    if W_ON:
        forward_weights()
    spread(splits - 1)
    if W_ON:
        for k in (1, 3, 2):
            f_copy(k).wait_recv()
    own_parts = [project(t) for t in range(splits)]
    for t in range(splits):
        finish(t, own_parts[t])

    for copy in kv:
        copy.wait_send()
    for t in range(splits):
        for o in range(1, GROUP):
            q_copy(t, o).wait_send()
            p_copy(t, o).wait_send()
        for k in (0, 1, 2, 3, 5, 6, 7):
            a_copy(t, k).wait_send()
        for k in range(1, 4):
            m_copy(t, k).wait_send()
    if W_ON:
        for k in range(1, 4):
            for z in range(NZH):
                w_copy(k, z).wait_send()
            f_copy(k).wait_send()


W_ON = True


def local(splits, q, lk, lv, ck, cv, windows, *args):
    width = TOK // splits
    hbm = pl.BlockSpec(memory_space=pltpu.HBM)
    dma = pltpu.SemaphoreType.DMA
    return pl.pallas_call(
        functools.partial(kernel, splits),
        out_shape=jax.ShapeDtypeStruct((FEAT, TOK), BF),
        in_specs=[hbm] * 12,
        out_specs=pl.BlockSpec(memory_space=pltpu.VMEM),
        scratch_shapes=[
            pltpu.VMEM((GROUP, TOK, HEAD), BF),
            pltpu.VMEM((4, FRAME, HEAD), BF),
            pltpu.VMEM((4, FRAME, HEAD), BF),
            pltpu.VMEM((4, HEAD, FRAME), BF),
            pltpu.VMEM((TOK, HEAD), BF),
            pltpu.VMEM((TOK, HEAD), BF),
            pltpu.VMEM((HEAD, TOK), BF),
            pltpu.VMEM((splits, GROUP, MSG, width), BF),
            pltpu.VMEM((splits, GROUP, MSG, width), BF),
            pltpu.VMEM((splits, 8, HEAD, width), BF),
            pltpu.VMEM((4, FEAT, COLS), BF),
            pltpu.VMEM((splits, 4, FEAT, width), BF),
            pltpu.VMEM((splits, 4, FEAT, width), BF),
            pltpu.VMEM((FEAT, TOK), BF),
            pltpu.VMEM((50, FEAT), F32),
            pltpu.VMEM((FEAT, 1), F32),
            pltpu.SMEM((4, 16), jnp.int32),
            pltpu.SMEM((16,), jnp.int32),
            pltpu.SMEM((32,), jnp.int32),
            pltpu.SMEM((1,), jnp.int32),
            dma((15,)),
            dma((2,)), dma((2,)),
            dma((splits, GROUP)), dma((splits, GROUP)),
            dma((splits, GROUP)), dma((splits, GROUP)),
            dma((splits, 8)), dma((splits, 8)),
            dma((4, NZH)), dma((4, NZH)),
            dma((4,)), dma((4,)),
            dma((splits, 4)), dma((splits, 4)),
        ],
        compiler_params=pltpu.CompilerParams(
            collective_id=0, has_side_effects=True, vmem_limit_bytes=60 << 20
        ),
        name="block_attention_projection",
    )(q, lk, lv, ck, cv, windows.T, *args)


def solution(mesh):
    return jax.shard_map(
        functools.partial(local, 2),
        mesh=mesh,
        in_specs=(
            P("frames", "heads"),
            P("frames", "heads"),
            P("frames", "heads"),
            P("frames", None, "heads"),
            P("frames", None, "heads"),
            P(),
            P(),
            P(),
            P("heads", "frames"),
            P("heads", None),
            P(None, "heads"),
            P(),
        ),
        out_specs=P("heads", "frames"),
        check_vma=False,
    )
```

time: 66.4 us -> 53.2 us (0.80)
  the two profiles are of different devices: /device:TPU:2 before, /device:TPU:4 now
where the time goes in v3:
time: 53.2 us; the launch traced here: 53.1 us
  Pallas kernels  50.9 us (96%)
  local copies, waits for them, and re-layouts  1.53 us (3%)
  between operations  0.66 us (1%)
    pallas_call x1, Pallas kernels, local(): pl.pallas_call(functools.partial(kernel, splits), out_shape=jax.ShapeDtyp...  50.9 us
    unnamed x1, local copies, waits for them, and re-layouts  1.53 us

profile of v3, /device:TPU:4, one launch (start us, length us, event | category | flops | bytes accessed | tf_op | source)
XLA Modules:
  0.0 53.1 jit_solution(1686967851000028053)
XLA Ops:
  0.7 50.9 %block_attention_projection.1 = bf16[160,256]{1,0:T(8,128)(2,1)} custom-call(bf16[256,128]{1,0:T(8,128)(2,1)} %q_hbm.1, bf16[256,128]{1,0:T(8,128)(2,1)} %lk_hbm.1, bf16[256,128]{1,0:T(8,128)(2,1)} %lv_hbm.1, bf16[2,512,128]{2,1,0:T(8,128)(2,1)} %ck_hbm.1, bf16[2,512,128]{2,1,0:T(8,128)(2,1)} %cv_hbm.1, s32[4,16]{1,0:T(4,128)} %bitcast.1, s32[16]{0:T(128)} %counts_hbm.1, ...), custom_call_target="tpu_custom_call" | custom-call | tf_op jit(solution)/shard_map/block_attention_projection/pallas_call | solution.py:288
  51.5 1.5 %copy.15 = bf16[160,256]{1,0:T(8,128)(2,1)} copy(bf16[160,256]{1,0:T(8,128)(2,1)} %block_attention_projection.1) | data formatting | bytes 163840

commit v4 on v3

--- a/solution.py
+++ b/solution.py
@@ -16,7 +16,6 @@
 TOK = 256
 FRAME = 512
 FEAT = 160
-HALF_FEAT = FEAT // 2
 COLS = 8 * HEAD
 MSG = HEAD + 16
 NEG = -(2.0**100)
@@ -40,24 +39,32 @@
     qall, kbuf, vbuf, vt, lk, lv, lvt, sent, came, att, wg, part, parts_in, resid, gate, gcol,
     windows, counts, slot_of, step,
     sem_load, sem_kv_s, sem_kv_r, sem_q_s, sem_q_r, sem_p_s, sem_p_r,
-    sem_a_s, sem_a_r, sem_w_s, sem_w_r, sem_f_s, sem_f_r, sem_m_s, sem_m_r,
+    sem_a_s, sem_a_r, sem_w_s, sem_w_r, sem_m_s, sem_m_r,
 ):
     zl, x, c, zh, y = coords()
     width = TOK // splits
+    even = 1 - c
     pair, side = y // 2, y % 2
+    my_set = even * pair + c * zh
+    my_slot = even * (2 * zh + side) + c * y
 
     def frame_peer(o, sign):
         dz, dx = o // NX, o % NX
         return device((zl + dz) % NZL, (x + sign * dx + NX) % NX, c, zh, y)
 
-    def z_peer(k):
-        return device(zl, x, c, (zh + k) % NZH, y)
+    def set_peer(k):
+        slot = (my_slot + k) % 8
+        return device(zl, x, c, even * (slot // 2) + c * zh, even * (2 * pair + slot % 2) + c * slot)
 
     def feature_peer(k):
-        return device(zl, x, c, zh, (y + 2 * k) % NY)
+        there = (my_set + k) % 4
+        return device(zl, x, c, even * zh + c * there, even * (2 * there + side) + c * y)
+
+    def columns(there, i):
+        start = (even * i + c * there) * 1024 + (even * there + c * i) * 256
+        return pl.ds(pl.multiple_of(start, 256), 256)
 
     other_core = device(zl, x, 1 - c, zh, y)
-    other_side = device(zl, x, c, zh, 2 * pair + 1 - side)
 
     mine = pl.ds(pl.multiple_of(c * 2, 2), 2)
     near = [
@@ -65,22 +72,18 @@
         (windows_hbm, windows), (counts_hbm, counts), (slots_hbm, slot_of), (step_hbm, step), (gate_hbm, gate),
         (res_hbm, resid),
     ]
-    for z in range(NZH):
-        near.append((
-            w_hbm.at[:, pl.ds(pl.multiple_of(z * 1024 + pair * 256, 256), 256)],
-            wg.at[pair, :, pl.ds(z * 256, 256)],
-        ))
+    for i in range(4):
+        near.append((w_hbm.at[:, columns(my_set, i)], wg.at[my_set, :, pl.ds(i * 256, 256)]))
     loads = [pltpu.make_async_copy(src, dst, sem_load.at[i]) for i, (src, dst) in enumerate(near)]
-    for load in loads:
-        load.start()
-
     barrier = pltpu.get_barrier_semaphore()
-    peers = [other_core, other_side]
-    peers += [frame_peer(o, 1) for o in range(1, GROUP)]
-    peers += [z_peer(k) for k in range(1, NZH)]
+    peers = [frame_peer(o, 1) for o in range(1, GROUP)]
+    peers += [other_core]
+    peers += [set_peer(k) for k in range(1, 8)]
     peers += [feature_peer(k) for k in range(1, 4)]
     for peer in peers:
         pl.semaphore_signal(barrier, inc=1, device_id=peer, device_id_type=MESH)
+    for load in loads:
+        load.start()
     pl.semaphore_wait(barrier, len(peers))
 
     def remote(src, dst, send, recv, peer):
@@ -105,39 +108,53 @@
         return remote(sent.at[t, o], came.at[t, o], sem_p_s.at[t, o], sem_p_r.at[t, o], frame_peer(o, -1))
 
     def a_copy(t, k):
-        here = att.at[t, 2 * ((zh + (0 if k < 4 else 8 - k)) % NZH) + side]
-        peer = z_peer(k) if 0 < k < 4 else other_side
-        return remote(here, here, sem_a_s.at[t, k], sem_a_r.at[t, k], peer)
-
-    rows = pl.ds(pl.multiple_of(c * HALF_FEAT, 16), HALF_FEAT)
-
-    def w_copy(k, z):
-        there = (pair + k) % 4
+        here = att.at[t, my_slot]
+        return remote(here, here, sem_a_s.at[t, k], sem_a_r.at[t, k], set_peer(k))
+
+    def w_copy(k, i):
         return remote(
-            w_hbm.at[rows, pl.ds(pl.multiple_of(z * 1024 + there * 256, 256), 256)],
-            wg.at[pair, rows, pl.ds(z * 256, 256)], sem_w_s.at[k, z], sem_w_r.at[k, z], feature_peer(k),
+            w_hbm.at[:, columns((my_set + k) % 4, i)],
+            wg.at[my_set, :, pl.ds(i * 256, 256)], sem_w_s.at[k, i], sem_w_r.at[k, i], feature_peer(k),
         )
 
-    def f_copy(k):
-        block = wg.at[(pair + 4 - k) % 4, rows]
-        return remote(block, block, sem_f_s.at[k], sem_f_r.at[k], other_core)
+    def quarter_copy(k):
+        return remote(
+            w_hbm.at[:, columns((my_set + k) % 4, x)],
+            wg.at[my_set, :, pl.ds(pl.multiple_of(x * 256, 256), 256)],
+            sem_w_s.at[k, 0], sem_w_r.at[k, 0], feature_peer(k),
+        )
+
+    def x_copy(k, d):
+        block = wg.at[(my_set + 4 - k) % 4, :, pl.ds(pl.multiple_of(x * 256, 256), 256)]
+        return remote(block, block, sem_w_s.at[k, d], sem_w_r.at[k, d], frame_peer(d, 1))
 
     def m_copy(t, k):
         return remote(part.at[t, k], parts_in.at[t, k], sem_m_s.at[t, k], sem_m_r.at[t, k], feature_peer(k))
 
-    q_order = [1, 4, 3, 2, 5, 7, 6]
     for copy in kv:
         copy.start()
+    first, second = [0, 1, 4, 3], [5, 7, 2, 6]
+    orders = (first + second, second[::-1] + first)
     for t in range(splits):
-        for o in q_order:
-            q_copy(t, o).start()
-    if W_ON:
-        for k in (2, 1, 3):
-            for z in range(NZH):
-                w_copy(k, z).start()
-
+        for o in orders[t]:
+            if o > 0:
+                q_copy(t, o).start()
     for load in loads:
         load.wait()
+
+    quarter_copy(2).start()
+
+    @pl.when(c == 0)
+    def _():
+        for k in (1, 3):
+            for i in range(4):
+                w_copy(k, i).start()
+
+    @pl.when(c == 1)
+    def _():
+        for k in (1, 3):
+            quarter_copy(k).start()
+
     lvt[...] = lv[...].T
     for i in range(2):
         vt[c * 2 + i] = vbuf[c * 2 + i].T
@@ -211,24 +228,19 @@
             share = jnp.exp2(stats[o][0:1] - m)
             total = total + share * (stats[o][1:2] + stats[o][2:3])
             result = result + share * (sent if o == 0 else came)[t, o, 0:HEAD].astype(F32)
-        att[t, 2 * zh + side] = (result / total).astype(BF)
-        for k in (2, 1, 3, 0):
+        att[t, my_slot] = (result / total).astype(BF)
+        for k in (4, 3, 5, 2, 6, 1, 7):
             a_copy(t, k).start()
 
-    def spread(t):
-        for k in (1, 3, 2):
-            a_copy(t, k).wait_recv()
-            a_copy(t, 4 + k).start()
-
     def project(t):
-        for k in (0, 5, 7, 6):
+        for k in range(1, 8):
             a_copy(t, k).wait_recv()
         rows_in = att[t].reshape(COLS, width)
         for k in (2, 1, 3):
-            mixed = jnp.dot(wg[(pair + k) % 4], rows_in, preferred_element_type=F32)
+            mixed = jnp.dot(wg[(my_set + k) % 4], rows_in, preferred_element_type=F32)
             part[t, k] = mixed.astype(BF)
             m_copy(t, k).start()
-        return jnp.dot(wg[pair], rows_in, preferred_element_type=F32)
+        return jnp.dot(wg[my_set], rows_in, preferred_element_type=F32)
 
     def finish(t, mixed):
         for k in (1, 3, 2):
@@ -236,27 +248,45 @@
             mixed = mixed + parts_in[t, k].astype(F32)
         out_ref[:, span(t)] = (resid[:, span(t)].astype(F32) + gcol[...] * mixed).astype(BF)
 
-    def forward_weights():
-        for k in (1, 3, 2):
-            for z in range(NZH):
-                w_copy(k, z).wait_recv()
-            f_copy(k).start()
-
-    first, second = [0, 1, 4, 3], [2, 5, 7, 6]
+    def share_weights():
+
+        def share(k):
+            quarter_copy(k).wait_recv()
+            for d in (2, 1, 3):
+                x_copy(k, d).start()
+
+        share(2)
+
+        @pl.when(c == 1)
+        def _():
+            share(1)
+            share(3)
+
+    def await_weights():
+
+        @pl.when(c == 0)
+        def _():
+            for k in (1, 3):
+                for i in range(4):
+                    w_copy(k, i).wait_recv()
+
+        @pl.when(c == 1)
+        def _():
+            for k in (1, 3):
+                for d in (1, 3, 2):
+                    x_copy(k, d).wait_recv()
+
+        for d in (1, 3, 2):
+            x_copy(2, d).wait_recv()
+
     visit(0, first)
     visit(0, second)
-    if splits == 2:
-        visit(1, first)
-        merge(0)
-        visit(1, second)
-        spread(0)
-    merge(splits - 1)
-    if W_ON:
-        forward_weights()
-    spread(splits - 1)
-    if W_ON:
-        for k in (1, 3, 2):
-            f_copy(k).wait_recv()
+    visit(1, second[::-1])
+    visit(1, first)
+    merge(0)
+    share_weights()
+    merge(1)
+    await_weights()
     own_parts = [project(t) for t in range(splits)]
     for t in range(splits):
         finish(t, own_parts[t])
@@ -267,18 +297,27 @@
         for o in range(1, GROUP):
             q_copy(t, o).wait_send()
             p_copy(t, o).wait_send()
-        for k in (0, 1, 2, 3, 5, 6, 7):
+        for k in range(1, 8):
             a_copy(t, k).wait_send()
         for k in range(1, 4):
             m_copy(t, k).wait_send()
-    if W_ON:
-        for k in range(1, 4):
-            for z in range(NZH):
-                w_copy(k, z).wait_send()
-            f_copy(k).wait_send()
-
-
-W_ON = True
+    def drain(k):
+        quarter_copy(k).wait_send()
+        for d in range(1, 4):
+            x_copy(k, d).wait_send()
+
+    drain(2)
+
+    @pl.when(c == 0)
+    def _():
+        for k in (1, 3):
+            for i in range(4):
+                w_copy(k, i).wait_send()
+
+    @pl.when(c == 1)
+    def _():
+        drain(1)
+        drain(3)
 
 
 def local(splits, q, lk, lv, ck, cv, windows, *args):
@@ -317,7 +356,6 @@
             dma((splits, GROUP)), dma((splits, GROUP)),
             dma((splits, 8)), dma((splits, 8)),
             dma((4, NZH)), dma((4, NZH)),
-            dma((4,)), dma((4,)),
             dma((splits, 4)), dma((splits, 4)),
         ],
         compiler_params=pltpu.CompilerParams(

time: 53.2 us -> 51.6 us (0.970)
  the two profiles are of different devices: /device:TPU:4 before, /device:TPU:1 now
where the time goes in v4:
time: 51.6 us; the launch traced here: 51.5 us
  Pallas kernels  49.3 us (96%)
  local copies, waits for them, and re-layouts  1.53 us (3%)
  between operations  0.66 us (1%)
    pallas_call x1, Pallas kernels, local(): pl.pallas_call(functools.partial(kernel, splits), out_shape=jax.ShapeDtyp...  49.3 us
    unnamed x1, local copies, waits for them, and re-layouts  1.53 us

profile of v4, /device:TPU:1, one launch (start us, length us, event | category | flops | bytes accessed | tf_op | source)
XLA Modules:
  0.0 51.5 jit_solution(3555137829109032407)
XLA Ops:
  0.7 49.3 %block_attention_projection.1 = bf16[160,256]{1,0:T(8,128)(2,1)} custom-call(bf16[256,128]{1,0:T(8,128)(2,1)} %q_hbm.1, bf16[256,128]{1,0:T(8,128)(2,1)} %lk_hbm.1, bf16[256,128]{1,0:T(8,128)(2,1)} %lv_hbm.1, bf16[2,512,128]{2,1,0:T(8,128)(2,1)} %ck_hbm.1, bf16[2,512,128]{2,1,0:T(8,128)(2,1)} %cv_hbm.1, s32[4,16]{1,0:T(4,128)} %bitcast.1, s32[16]{0:T(128)} %counts_hbm.1, ...), custom_call_target="tpu_custom_call" | custom-call | tf_op jit(solution)/shard_map/block_attention_projection/pallas_call | solution.py:327
  49.9 1.5 %copy.15 = bf16[160,256]{1,0:T(8,128)(2,1)} copy(bf16[160,256]{1,0:T(8,128)(2,1)} %block_attention_projection.1) | data formatting | bytes 163840

commit v5 on v4

--- a/solution.py
+++ b/solution.py
@@ -229,18 +229,28 @@
             total = total + share * (stats[o][1:2] + stats[o][2:3])
             result = result + share * (sent if o == 0 else came)[t, o, 0:HEAD].astype(F32)
         att[t, my_slot] = (result / total).astype(BF)
-        for k in (4, 3, 5, 2, 6, 1, 7):
-            a_copy(t, k).start()
+        for slot in range(8):
+
+            @pl.when(slot != my_slot)
+            def _():
+                a_copy(t, (slot - my_slot + 8) % 8).start()
 
     def project(t):
         for k in range(1, 8):
             a_copy(t, k).wait_recv()
-        rows_in = att[t].reshape(COLS, width)
-        for k in (2, 1, 3):
-            mixed = jnp.dot(wg[(my_set + k) % 4], rows_in, preferred_element_type=F32)
-            part[t, k] = mixed.astype(BF)
-            m_copy(t, k).start()
-        return jnp.dot(wg[my_set], rows_in, preferred_element_type=F32)
+
+        def product(there):
+            return jnp.dot(wg[there], att[t].reshape(COLS, width), preferred_element_type=F32)
+
+        for there in range(4):
+
+            @pl.when(there != my_set)
+            def _():
+                k = (there - my_set + 4) % 4
+                part[t, k] = product(there).astype(BF)
+                m_copy(t, k).start()
+
+        return product(my_set)
 
     def finish(t, mixed):
         for k in (1, 3, 2):
@@ -283,8 +293,8 @@
     visit(0, second)
     visit(1, second[::-1])
     visit(1, first)
+    share_weights()
     merge(0)
-    share_weights()
     merge(1)
     await_weights()
     own_parts = [project(t) for t in range(splits)]

time: 51.6 us -> 50.2 us (0.973)
  Pallas kernels: 49.3 us -> 47.8 us
    pallas_call x1, Pallas kernels: 49.3 us -> 47.8 us  [local(): pl.pallas_call(functools.partial(kernel, splits), out_shape=jax.ShapeDtyp...]
where the time goes in v5:
time: 50.2 us; the launch traced here: 50 us
  Pallas kernels  47.8 us (95%)
  local copies, waits for them, and re-layouts  1.53 us (3%)
  between operations  0.66 us (1%)
    pallas_call x1, Pallas kernels, local(): pl.pallas_call(functools.partial(kernel, splits), out_shape=jax.ShapeDtyp...  47.8 us
    unnamed x1, local copies, waits for them, and re-layouts  1.53 us

profile of v5, /device:TPU:1, one launch (start us, length us, event | category | flops | bytes accessed | tf_op | source)
XLA Modules:
  0.0 50.0 jit_solution(1496780828106824974)
XLA Ops:
  0.7 47.8 %block_attention_projection.1 = bf16[160,256]{1,0:T(8,128)(2,1)} custom-call(bf16[256,128]{1,0:T(8,128)(2,1)} %q_hbm.1, bf16[256,128]{1,0:T(8,128)(2,1)} %lk_hbm.1, bf16[256,128]{1,0:T(8,128)(2,1)} %lv_hbm.1, bf16[2,512,128]{2,1,0:T(8,128)(2,1)} %ck_hbm.1, bf16[2,512,128]{2,1,0:T(8,128)(2,1)} %cv_hbm.1, s32[4,16]{1,0:T(4,128)} %bitcast.1, s32[16]{0:T(128)} %counts_hbm.1, ...), custom_call_target="tpu_custom_call" | custom-call | tf_op jit(solution)/shard_map/block_attention_projection/pallas_call | solution.py:337
  48.5 1.5 %copy.15 = bf16[160,256]{1,0:T(8,128)(2,1)} copy(bf16[160,256]{1,0:T(8,128)(2,1)} %block_attention_projection.1) | data formatting | bytes 163840

commit v6 on v5

--- a/solution.py
+++ b/solution.py
@@ -35,10 +35,10 @@
 def kernel(
     splits,
     q_hbm, lk_hbm, lv_hbm, ck_hbm, cv_hbm, windows_hbm, counts_hbm, slots_hbm, res_hbm, w_hbm, gate_hbm, step_hbm,
-    out_ref,
-    qall, kbuf, vbuf, vt, lk, lv, lvt, sent, came, att, wg, part, parts_in, resid, gate, gcol,
+    out_hbm,
+    qall, kbuf, vbuf, vt, lk, lv, lvt, sent, came, att, wg, part, parts_in, resid, gate, gcol, updated,
     windows, counts, slot_of, step,
-    sem_load, sem_kv_s, sem_kv_r, sem_q_s, sem_q_r, sem_p_s, sem_p_r,
+    sem_load, sem_out, sem_kv_s, sem_kv_r, sem_q_s, sem_q_r, sem_p_s, sem_p_r,
     sem_a_s, sem_a_r, sem_w_s, sem_w_r, sem_m_s, sem_m_r,
 ):
     zl, x, c, zh, y = coords()
@@ -82,7 +82,8 @@
     peers += [feature_peer(k) for k in range(1, 4)]
     for peer in peers:
         pl.semaphore_signal(barrier, inc=1, device_id=peer, device_id_type=MESH)
-    for load in loads:
+    early, late = loads[:9], loads[9:]
+    for load in early:
         load.start()
     pl.semaphore_wait(barrier, len(peers))
 
@@ -139,7 +140,9 @@
         for o in orders[t]:
             if o > 0:
                 q_copy(t, o).start()
-    for load in loads:
+    for load in late:
+        load.start()
+    for load in early:
         load.wait()
 
     quarter_copy(2).start()
@@ -158,8 +161,6 @@
     lvt[...] = lv[...].T
     for i in range(2):
         vt[c * 2 + i] = vbuf[c * 2 + i].T
-    hot = lax.broadcasted_iota(jnp.int32, gate.shape, 0) == step[0]
-    gcol[...] = jnp.sum(jnp.where(hot, gate[...], 0.0).T, axis=1, keepdims=True)
     for copy in kv:
         copy.wait_recv()
     for i in range(2):
@@ -256,7 +257,7 @@
         for k in (1, 3, 2):
             m_copy(t, k).wait_recv()
             mixed = mixed + parts_in[t, k].astype(F32)
-        out_ref[:, span(t)] = (resid[:, span(t)].astype(F32) + gcol[...] * mixed).astype(BF)
+        updated[:, span(t)] = (resid[:, span(t)].astype(F32) + gcol[...] * mixed).astype(BF)
 
     def share_weights():
 
@@ -294,12 +295,20 @@
     visit(1, second[::-1])
     visit(1, first)
     share_weights()
+    for load in late:
+        load.wait()
+    hot = lax.broadcasted_iota(jnp.int32, gate.shape, 0) == step[0]
+    gcol[...] = jnp.sum(jnp.where(hot, gate[...], 0.0).T, axis=1, keepdims=True)
     merge(0)
     merge(1)
     await_weights()
     own_parts = [project(t) for t in range(splits)]
+    outs = [
+        pltpu.make_async_copy(updated.at[:, span(t)], out_hbm.at[:, span(t)], sem_out.at[t]) for t in range(splits)
+    ]
     for t in range(splits):
         finish(t, own_parts[t])
+        outs[t].start()
 
     for copy in kv:
         copy.wait_send()
@@ -317,6 +326,8 @@
             x_copy(k, d).wait_send()
 
     drain(2)
+    for out in outs:
+        out.wait()
 
     @pl.when(c == 0)
     def _():
@@ -338,7 +349,7 @@
         functools.partial(kernel, splits),
         out_shape=jax.ShapeDtypeStruct((FEAT, TOK), BF),
         in_specs=[hbm] * 12,
-        out_specs=pl.BlockSpec(memory_space=pltpu.VMEM),
+        out_specs=hbm,
         scratch_shapes=[
             pltpu.VMEM((GROUP, TOK, HEAD), BF),
             pltpu.VMEM((4, FRAME, HEAD), BF),
@@ -356,11 +367,13 @@
             pltpu.VMEM((FEAT, TOK), BF),
             pltpu.VMEM((50, FEAT), F32),
             pltpu.VMEM((FEAT, 1), F32),
+            pltpu.VMEM((FEAT, TOK), BF),
             pltpu.SMEM((4, 16), jnp.int32),
             pltpu.SMEM((16,), jnp.int32),
             pltpu.SMEM((32,), jnp.int32),
             pltpu.SMEM((1,), jnp.int32),
             dma((15,)),
+            dma((splits,)),
             dma((2,)), dma((2,)),
             dma((splits, GROUP)), dma((splits, GROUP)),
             dma((splits, GROUP)), dma((splits, GROUP)),

time: 50.2 us -> 50.1 us (level)
  no operation moved by 1% of the time
where the time goes in v6:
time: 50.1 us; the launch traced here: 49.9 us
  Pallas kernels  47.7 us (95%)
  local copies, waits for them, and re-layouts  1.53 us (3%)
  between operations  0.66 us (1%)
    pallas_call x1, Pallas kernels, local(): pl.pallas_call(functools.partial(kernel, splits), out_shape=jax.ShapeDtyp...  47.7 us
    unnamed x1, local copies, waits for them, and re-layouts  1.53 us

profile of v6, /device:TPU:1, one launch (start us, length us, event | category | flops | bytes accessed | tf_op | source)
XLA Modules:
  0.0 49.9 jit_solution(12796396699973699200)
XLA Ops:
  0.7 47.7 %block_attention_projection.1 = bf16[160,256]{1,0:T(8,128)(2,1)} custom-call(bf16[256,128]{1,0:T(8,128)(2,1)} %q_hbm.1, bf16[256,128]{1,0:T(8,128)(2,1)} %lk_hbm.1, bf16[256,128]{1,0:T(8,128)(2,1)} %lv_hbm.1, bf16[2,512,128]{2,1,0:T(8,128)(2,1)} %ck_hbm.1, bf16[2,512,128]{2,1,0:T(8,128)(2,1)} %cv_hbm.1, s32[4,16]{1,0:T(4,128)} %bitcast.1, s32[16]{0:T(128)} %counts_hbm.1, ...), custom_call_target="tpu_custom_call" | custom-call | tf_op jit(solution)/shard_map/block_attention_projection/pallas_call | solution.py:348
  48.4 1.5 %copy.15 = bf16[160,256]{1,0:T(8,128)(2,1)} copy(bf16[160,256]{1,0:T(8,128)(2,1)} %block_attention_projection.1) | data formatting | bytes 163840
